TPU v7x, 32 devices: a whole 2x2x4 slice. The times are simulated.
32 devices in a mesh: grp: 2 (over y), ct: 4 (over z), tm: 2 (over x), pol: 2 (over core).
Axes of the slice: x: 2, y: 2, z: 4, core: 2. Of those that a mesh axis runs over, the one named last changes fastest.
Arguments:
- voltages: bfloat16 [2048, 98304], P(('grp', 'ct', 'pol'), 'tm'), parts along dimension 0, may hold values from -4 to 4
- pfb_coeffs: float32 [4, 16384], replicated, may hold values from -3 to 3
- beam_delays: float32 [4, 1024], replicated, may hold values from -512 to 512
- slot_of_input: int32 [1024], replicated, may hold values from 0 to 1023, each once
- block_list: int32 [2, 2], replicated, may hold values from 0 to 15, as said below
Outputs:
- visibilities: bfloat16 [64, 4, 2, 64, 8192], P('tm', 'grp', None, None, ('ct', 'pol')), parts along dimension 1
- beams: bfloat16 [8, 6, 2, 8192], P('grp', 'tm', None, ('ct', 'pol')), parts along dimension 0
There are 2 independent parts, one for each index of `grp`. A program takes and returns all parts, laid end to end along the dimension named above; an argument that names none is the same for every part. Nothing has to cross between parts.
Inputs may be any that keep to these rules, and one draw needn't show every extreme that they name: slot_of_input holds every number below 1024 once. `block_list`: each pair is a block row and a block column of 64-input groups with the row at least the column; the first pair lies in the last block row and the last pair in the first block column.
All inputs are finite; a program needn't handle non-finite values.
Results may differ from a plain program's by a relative error of at most 0.011.
Values may be sent and summed in bfloat16 or wider, within the bound.
A program may use at most 320 MiB of HBM per device.

v0:
```python
import math

import jax
import jax.numpy as jnp
from jax import lax
from jax.sharding import PartitionSpec as P

NCH = 8192
BLK = 64
FFT_A = 128
FFT_B = 128


def shifted(block, axis, distance):
    devices = range(lax.axis_size(axis))
    route = [(i - distance, i) for i in devices if i - distance in devices]
    return lax.ppermute(block, axis, route)


def make_tables(first_len, second_len):
    frame_len = first_len * second_len
    half_len = second_len // 2
    rows_a = jnp.arange(first_len, dtype=jnp.int32)
    phase_a = (rows_a[:, None] * rows_a[None, :] % first_len).astype(jnp.float32) * (
        2.0 * math.pi / first_len
    )
    first_table = (jnp.stack([jnp.cos(phase_a), -jnp.sin(phase_a)]) * first_len ** (-0.5)).astype(
        jnp.bfloat16
    )
    cols_b = jnp.arange(second_len, dtype=jnp.int32)
    phase_t = (rows_a[:, None] * cols_b[None, :] % frame_len).astype(jnp.float32) * (
        2.0 * math.pi / frame_len
    )
    twist_re = jnp.cos(phase_t)
    twist_im = -jnp.sin(phase_t)
    rows_h = jnp.arange(half_len, dtype=jnp.int32)
    phase_b = (rows_h[:, None] * cols_b[None, :] % second_len).astype(jnp.float32) * (
        2.0 * math.pi / second_len
    )
    cos_b = jnp.cos(phase_b) * second_len ** (-0.5)
    sin_b = -jnp.sin(phase_b) * second_len ** (-0.5)
    second = jnp.stack([jnp.stack([cos_b, -sin_b]), jnp.stack([sin_b, cos_b])]).astype(jnp.bfloat16)
    return (first_table, twist_re, twist_im, second)


def settle(values):
    return lax.optimization_barrier(values.astype(jnp.bfloat16)).astype(jnp.float32)


def on_device(voltages, pfb_coeffs, beam_delays, slot_of_input, block_list):
    tap_count = pfb_coeffs.shape[0]
    rows_dev = voltages.shape[0]
    frame_len = pfb_coeffs.shape[1]
    spectra_dev = voltages.shape[1] // frame_len
    frames = voltages.reshape(rows_dev, spectra_dev, frame_len)
    earlier = shifted(frames, "tm", 1)
    extended = jnp.concatenate([earlier, frames], axis=1)
    filtered = jnp.zeros((rows_dev, spectra_dev, frame_len), jnp.float32)
    for tap_index in range(tap_count):
        filtered = filtered + pfb_coeffs[tap_index][None, None, :] * extended[
            :, tap_index : tap_index + spectra_dev
        ].astype(jnp.float32)
    first_table, twist_re, twist_im, second = make_tables(FFT_A, FFT_B)
    shaped = filtered.astype(jnp.bfloat16).reshape(rows_dev, spectra_dev, FFT_A, FFT_B)
    section_one = jnp.einsum(
        "ckn,rsnm->rsckm", first_table, shaped, preferred_element_type=jnp.float32
    )
    real_part = section_one[:, :, 0] * twist_re - section_one[:, :, 1] * twist_im
    imag_part = section_one[:, :, 0] * twist_im + section_one[:, :, 1] * twist_re
    twisted = jnp.stack([real_part, imag_part], 2).astype(jnp.bfloat16)
    shards = lax.axis_size("ct") * lax.axis_size("pol")
    half_len = FFT_B // 2
    second_split = second.reshape(2, 2, shards, half_len // shards, FFT_B)
    outgoing = jnp.einsum(
        "ocdqm,rsckm->drsoqk", second_split, twisted, preferred_element_type=jnp.float32
    ).astype(jnp.bfloat16)
    channel_count = NCH // shards
    outgoing = outgoing.reshape(shards, rows_dev, spectra_dev, 2, channel_count)
    inputs_all = shards * rows_dev
    arrived = lax.all_to_all(outgoing, ("ct", "pol"), split_axis=0, concat_axis=0, tiled=True)
    spectra = arrived.reshape(inputs_all, spectra_dev, 2, channel_count)
    first_channel = (
        lax.axis_index("ct") * lax.axis_size("pol") + lax.axis_index("pol")
    ) * channel_count
    channels = (first_channel + jnp.arange(channel_count, dtype=jnp.int32)).astype(jnp.float32)
    ratio = NCH / (NCH + channels)
    delays_slot = jnp.zeros_like(beam_delays).at[:, slot_of_input].set(beam_delays)
    phases = delays_slot[:, :, None] * ratio[None, None, :] * (2.0 * math.pi)
    norm_scale = inputs_all ** (-0.5)
    weight_re = (jnp.cos(phases) * norm_scale).astype(jnp.bfloat16)
    weight_im = (-jnp.sin(phases) * norm_scale).astype(jnp.bfloat16)
    weights = jnp.stack(
        [jnp.stack([weight_re, -weight_im], 1), jnp.stack([weight_im, weight_re], 1)], 1
    )
    beams = jnp.einsum(
        "eozlk,lszk->esok", weights, spectra, preferred_element_type=jnp.float32
    ).astype(jnp.bfloat16)
    block_len = BLK

    def select_rows(group_index):
        slots = lax.dynamic_slice_in_dim(slot_of_input, group_index * block_len, block_len)
        return jnp.take(spectra, slots, axis=0)

    left_rows = jax.vmap(select_rows)(block_list[:, 0])
    right_rows = jax.vmap(select_rows)(block_list[:, 1])
    swapped = jnp.stack([-right_rows[:, :, :, 1], right_rows[:, :, :, 0]], 3)
    paired = jnp.stack([right_rows, swapped], 1)
    summed = lax.psum_scatter(
        settle(
            jnp.einsum("biszk,bojszk->ibojk", left_rows, paired, preferred_element_type=jnp.float32)
        ).astype(jnp.bfloat16),
        "tm",
        scatter_dimension=0,
        tiled=True,
    )
    return (summed, beams)


def solution(mesh):
    return jax.shard_map(
        on_device,
        mesh=mesh,
        in_specs=(P(("grp", "ct", "pol"), "tm"), P(), P(), P(), P()),
        out_specs=(P("tm", "grp", None, None, ("ct", "pol")), P("grp", "tm", None, ("ct", "pol"))),
        check_vma=False,
    )
```

profile of v0, /device:TPU:0, one launch (start us, length us, event | category | flops | bytes accessed | tf_op | source)
XLA Modules:
  0.0 1331.7 jit_solution(421094336617466146)
XLA Ops:
  7.2 16.6 %copy.103 = bf16[128,49152]{0,1:T(8,128)(2,1)} copy(bf16[128,49152]{1,0:T(8,128)(2,1)} %param.7) | data formatting | bytes 25165824 | tf_op args[0]
  23.8 5.6 collective-permute-start
  29.5 0.3 sine_negate_fusion.1
  30.4 268.1 %collective-permute-done = bf16[128,3,16384]{0,2,1:T(8,128)(2,1)S(1)} collective-permute-done((bf16[128,3,16384]{0,2,1:T(8,128)(2,1)}, bf16[128,3,16384]{0,2,1:T(8,128)(2,1)S(1)}, u32[]{:S(2)}, u32[]{:S(2)}) %collective-permute-start) | collective-permute-done | bytes 12582944 | tf_op jit(solution)/shard_map/ppermute | solution.py:17
  298.5 17.8 %add_convert_fusion.1 = bf16[128,3,16384]{0,2,1:T(8,128)(2,1)} fusion(bf16[128,3,16384]{0,2,1:T(8,128)(2,1)} %bitcast.95, bf16[128,3,16384]{0,2,1:T(8,128)(2,1)S(1)} %collective-permute-done, f32[16384]{0:T(1024)S(1)} %bitcast.101, f32[16384]{0:T(1024)S(1)} %bitcast.102, f32[16384]{0:T(1024)S(1)} %bitcast.100, f32[16384]{0:T(1024)S(1)} %bitcast.99), kind=kLoop, calls=%fused_computation.19 | loop fusion | flops 88080384 | bytes 38010880 | tf_op jit(solution)/shard_map/convert_element_type | solution.py:64
  316.3 17.6 %copy.122 = bf16[128,3,128,128,1]{2,3,4,1,0:T(8,128)(2,1)} copy(bf16[128,3,128,128,1]{0,3,2,1,4:T(8,128)(2,1)} %bitcast.96) | data formatting | bytes 25165824 | tf_op jit(solution)/shard_map/reshape | solution.py:64
  333.9 21.7 %convolution_bitcast_fusion = f32[128,3,2,128,128]{3,4,2,1,0:T(8,128)} fusion(bf16[128,3,128,128,1]{2,3,4,1,0:T(8,128)(2,1)} %copy.122, f32[1,128,128]{2,1,0:T(8,128)S(1)} %get-tuple-element.64, f32[1,128,128]{2,1,0:T(8,128)S(1)} %get-tuple-element.65), kind=kOutput, calls=%fused_computation.20 | convolution fusion | flops 3221323776 | bytes 63045632 | tf_op jit(solution)/shard_map/ckn,rsnm->rsckm/dot_general | solution.py:65
  355.6 21.3 %subtract_convert_fusion = (bf16[128,3,1,128,128]{3,4,2,1,0:T(8,128)(2,1)S(1)}, bf16[128,3,1,128,128]{3,4,2,1,0:T(8,128)(2,1)}) fusion(f32[128,3,2,128,128]{3,4,2,1,0:T(8,128)} %convolution_bitcast_fusion, f32[128,128]{0,1:T(8,128)S(1)} %get-tuple-element.66, f32[128,128]{0,1:T(8,128)S(1)} %get-tuple-element.67), kind=kLoop, calls=%fused_computation.18 | loop fusion | flops 50331648 | bytes 75628544 | tf_op jit(solution)/shard_map/convert.6
  377.0 9.1 fusion.4
  386.1 19.2 %reshape.275 = bf16[8,128,3,2,1024]{4,0,3,2,1:T(8,128)(2,1)} reshape(bf16[8,128,3,2,8,128]{5,4,0,3,2,1:T(8,128)(2,1)} %fusion.4) | data formatting | bytes 25165824 | tf_op jit(solution)/shard_map/reshape | solution.py:78
  405.3 14.6 %copy.106 = bf16[8,128,3,2,1024]{4,1,3,2,0:T(8,128)(2,1)} copy(bf16[8,128,3,2,1024]{4,0,3,2,1:T(8,128)(2,1)} %reshape.275) | data formatting | bytes 25165824 | tf_op jit(solution)/shard_map/reshape | solution.py:78
  419.9 5.5 all-to-all-start
  425.4 0.3 reduce-scatter.2.cloned.1.call-start
  425.9 2.6 while.2
  425.9 0.6 constant_dynamic-slice_fusion.4
  426.5 0.7 dynamic-slice_bitcast_fusion.4
  427.2 0.6 constant_dynamic-slice_fusion.4
  427.8 0.7 dynamic-slice_bitcast_fusion.4
  428.7 2.7 while.3
  428.7 0.6 constant_dynamic-slice_fusion.5
  429.3 0.7 dynamic-slice_bitcast_fusion.5
  430.0 0.6 constant_dynamic-slice_fusion.5
  430.6 0.7 dynamic-slice_bitcast_fusion.5
  431.5 267.6 %all-to-all-done = bf16[8,128,3,2,1024]{4,1,3,2,0:T(8,128)(2,1)} async-done(((bf16[8,128,3,2,1024]{4,1,3,2,0:T(8,128)(2,1)}), bf16[8,128,3,2,1024]{4,1,3,2,0:T(8,128)(2,1)}, u32[]{:S(2)}, u32[]{:S(2)}) %all-to-all-start) | async-done | bytes 12582944 | tf_op jit(solution)/shard_map/all_to_all | solution.py:80
  699.1 6.3 copy.107
  705.5 4.5 copy-done
  710.0 40.0 %copy.108 = bf16[1024,3,2,1024]{3,1,2,0:T(4,128)(2,1)} copy(bf16[1024,3,2,1024]{3,0,2,1:T(8,128)(2,1)S(1)} %bitcast.92) | data formatting | bytes 25165824 | tf_op jit(solution)/shard_map/reshape | solution.py:81
  750.0 8.1 gather_fusion
  758.1 5.4 copy.110
  763.4 6.0 fusion.54
  769.4 6.0 broadcast_select_fusion
  775.4 8.1 gather_fusion.1
  783.5 1.1 copy.114
  784.9 4.8 copy.127
  789.7 3.2 slice_negate_fusion
  792.8 5.5 maximum_bitcast_fusion.6
  798.3 41.0 %fusion = bf16[64,2,2,64,1024]{0,3,2,4,1:T(8,128)(2,1)} fusion(bf16[2,64,3,2,1024,1]{1,2,3,5,4,0:T(4,128)(2,1)} %copy.127, bf16[2,1,64,3,2,1024]{2,3,4,1,5,0:T(4,128)(2,1)} %maximum_bitcast_fusion.6, bf16[2,1,64,3,2,1024]{2,3,4,1,5,0:T(4,128)(2,1)} %fusion.54), kind=kOutput, calls=%fused_computation.8 | convolution fusion | flops 224395264 | bytes 38273024 | tf_op jit(solution)/shard_map/biszk,bojszk->ibojk/dot_general | solution.py:110
  839.4 84.0 %copy.116 = bf16[64,2,2,64,1024]{4,3,2,1,0:T(8,128)(2,1)} copy(bf16[64,2,2,64,1024]{0,3,2,4,1:T(8,128)(2,1)} %fusion) | data formatting | bytes 67108864 | tf_op jit(solution)/shard_map/optimization_barrier | solution.py:47
  923.4 0.7 copy-done.2
  924.3 3.2 scatter_custom_fusion
  927.7 58.5 %fusion.10 = bf16[4,1,1024,1024]{3,2,1,0:T(8,128)(2,1)S(1)} fusion(f32[1024]{0:T(1024)S(1)} %add_divide_fusion, f32[4,1024]{1,0:T(4,128)S(1)} %copy.118), kind=kLoop, calls=%fused_computation.38 | loop fusion | flops 33554432 | bytes 8409088 | tf_op jit(solution)/shard_map/neg | solution.py:93
  986.2 63.7 %multiply_convert_fusion = (bf16[4,1,1024,1024]{3,2,1,0:T(8,128)(2,1)S(1)}, bf16[4,1,1024,1024]{3,2,1,0:T(8,128)(2,1)S(1)}) fusion(f32[1024]{0:T(1024)S(1)} %add_divide_fusion, f32[4,1024]{1,0:T(4,128)S(1)} %copy.118), kind=kLoop, calls=%fused_computation.23 | loop fusion | flops 29360128 | bytes 16797696 | tf_op jit(solution)/shard_map/convert_element_type | solution.py:91
  1049.9 11.4 maximum_bitcast_fusion.2
  1061.4 23.4 %pad_maximum_fusion = bf16[4,2,2,1024,1024]{4,3,2,0,1:T(8,128)(2,1)} fusion(bf16[4,1,2,1024,1024]{4,3,2,0,1:T(8,128)(2,1)} %get-tuple-element.50, bf16[4,1,2,1024,1024]{4,3,2,0,1:T(8,128)(2,1)} %get-tuple-element.49), kind=kLoop, calls=%fused_computation.9 | loop fusion | flops 16777216 | bytes 67108864 | tf_op jit(solution)/shard_map/stack | solution.py:92
  1084.8 56.5 %copy.120 = bf16[4,2,2,1024,1024]{3,0,2,1,4:T(4,128)(2,1)} copy(bf16[4,2,2,1024,1024]{4,3,2,0,1:T(8,128)(2,1)} %pad_maximum_fusion) | data formatting | bytes 67108864 | tf_op jit(solution)/shard_map/stack | solution.py:92
  1141.3 27.7 %copy.129 = bf16[1024,3,2,1024,1]{0,1,2,4,3:T(4,128)(2,1)} copy(bf16[1024,3,2,1024,1]{3,0,2,1,4:T(8,128)(2,1)} %bitcast.93) | data formatting | bytes 25165824 | tf_op jit(solution)/shard_map/reshape | solution.py:81
  1168.9 153.4 %fusion.9 = bf16[4,3,2,1024]{0,1,2,3:T(4,128)(2,1)S(1)} fusion(bf16[1024,3,2,1024,1]{0,1,2,4,3:T(4,128)(2,1)} %copy.129, bf16[4,2,2,1024,1024]{3,0,2,1,4:T(4,128)(2,1)} %copy.120), kind=kOutput, calls=%fused_computation.36 | convolution fusion | flops 100687872 | bytes 46186496 | tf_op jit(solution)/shard_map/eozlk,lszk->esok/dot_general | solution.py:95
  1322.4 2.1 copy.121
  (38 shorter events, 2.0 us)
Async XLA Ops:
  7.2 23.1 %copy-start.1 = (f32[4,16384]{1,0:T(4,128)S(1)}, f32[4,16384]{1,0:T(4,128)}, u32[]{:S(2)}) copy-start(f32[4,16384]{1,0:T(4,128)} %param.8) | copy-start | bytes 786436
  23.8 274.7 %collective-permute-start = (bf16[128,3,16384]{0,2,1:T(8,128)(2,1)}, bf16[128,3,16384]{0,2,1:T(8,128)(2,1)S(1)}, u32[]{:S(2)}, u32[]{:S(2)}) collective-permute-start(bf16[128,3,16384]{0,2,1:T(8,128)(2,1)} %bitcast.94), channel_id=1, source_target_pairs={{0,2},{1,3},{4,6},{5,7},{8,10},{9,11},{12,14},{13,15},{16,18},{17,... | collective-permute-start | bytes 37748744 | tf_op jit(solution)/shard_map/ppermute | solution.py:17
  419.9 5.8 copy-start.4
  419.9 6.0 copy-start.3
  419.9 279.3 %all-to-all-start = ((bf16[8,128,3,2,1024]{4,1,3,2,0:T(8,128)(2,1)}), bf16[8,128,3,2,1024]{4,1,3,2,0:T(8,128)(2,1)}, u32[]{:S(2)}, u32[]{:S(2)}) async-start(bf16[8,128,3,2,1024]{4,1,3,2,0:T(8,128)(2,1)} %copy.106), calls=%async_computation | async-start | bytes 25165824 | tf_op jit(solution)/shard_map/all_to_all | solution.py:80
  425.4 899.1 %reduce-scatter.2.cloned.1.call-start = ((), (), s32[]{:S(2)}) async-start(), calls=%async_computation.2 | async-start | bytes 50331648 | tf_op jit(solution)/shard_map/reduce_scatter | solution.py:108
  705.5 4.5 copy-start
  923.4 0.7 copy-start.2
Sparse Core Ops, SparseCore 0:
  923.5 368.6 reduce-scatter.1
where the time goes:
time: 1350 us; the launch traced here: 1330 us
  waiting for transfers between devices  536 us (40%)
  local copies, waits for them, and re-layouts  327 us (24%)
  matrix products  225 us (17%)
  other arithmetic  218 us (16%)
  between operations  14.6 us (1%)
    ppermute x1, waiting for transfers between devices, shifted(): return lax.ppermute(block, axis, route)  268 us
    all_to_all x1, waiting for transfers between devices, on_device(): lax.all_to_all(outgoing, ('ct', 'pol'), split_axis=0, concat_axis=0, tile...  268 us
    dot_general x1, matrix products, on_device(): jnp.einsum('eozlk,lszk->esok', weights, spectra, preferred_element_type=j...  153 us
    optimization_barrier x1, local copies, waits for them, and re-layouts, settle(): lax.optimization_barrier(values.astype(jnp.bfloat16)).astype(jnp.float32)  84 us
    reshape x2, local copies, waits for them, and re-layouts, on_device(): spectra = arrived.reshape(inputs_all, spectra_dev, 2, channel_count)  67.6 us
    convert_element_type x1, other arithmetic, on_device(): weight_im = (-jnp.sin(phases) * norm_scale).astype(jnp.bfloat16)  63.7 us
    neg x1, other arithmetic, on_device(): -weight_im  58.5 us
    another operation x1, local copies, waits for them, and re-layouts, on_device(): jnp.stack([jnp.stack([weight_re, -weight_im], 1), jnp.stack([weight_im, w...  56.5 us
  transfers between devices with their start and end apart: 3, of which 2 were waited for; matrix products, arithmetic and copies ran while one was open for 31% of the time, Pallas kernels for 0%

commit v1 on v0

v1 whole, which is shorter than its diff:
```python
import math

import jax
import jax.numpy as jnp
from jax import lax
from jax.experimental import pallas as pl
from jax.experimental.pallas import tpu as pltpu
from jax.sharding import PartitionSpec as P

NCH = 8192
BLK = 64
FFT_A = 128
FFT_B = 128


def shifted(block, axis, distance):
    devices = range(lax.axis_size(axis))
    route = [(i - distance, i) for i in devices if i - distance in devices]
    return lax.ppermute(block, axis, route)


def make_tables(first_len, second_len):
    frame_len = first_len * second_len
    half_len = second_len // 2
    rows_a = jnp.arange(first_len, dtype=jnp.int32)
    phase_a = (rows_a[:, None] * rows_a[None, :] % first_len).astype(jnp.float32) * (
        2.0 * math.pi / first_len
    )
    first_table = (jnp.stack([jnp.cos(phase_a), -jnp.sin(phase_a)]) * first_len ** (-0.5)).astype(
        jnp.bfloat16
    )
    cols_b = jnp.arange(second_len, dtype=jnp.int32)
    phase_t = (rows_a[:, None] * cols_b[None, :] % frame_len).astype(jnp.float32) * (
        2.0 * math.pi / frame_len
    )
    twist_re = jnp.cos(phase_t)
    twist_im = -jnp.sin(phase_t)
    rows_h = jnp.arange(half_len, dtype=jnp.int32)
    phase_b = (rows_h[:, None] * cols_b[None, :] % second_len).astype(jnp.float32) * (
        2.0 * math.pi / second_len
    )
    cos_b = jnp.cos(phase_b) * second_len ** (-0.5)
    sin_b = -jnp.sin(phase_b) * second_len ** (-0.5)
    second = jnp.stack([jnp.stack([cos_b, -sin_b]), jnp.stack([sin_b, cos_b])]).astype(jnp.bfloat16)
    return (first_table, twist_re, twist_im, second)


def beam_kernel(weight_re_ref, weight_im_ref, spectra_ref, out_ref):
    beam_count, shards, rows, lanes = weight_re_ref.shape
    step = 16
    for lane in range(0, lanes, 128):
        cols = pl.ds(lane, 128)

        def add(t, totals):
            d = t // (rows // step)
            at = pl.ds(pl.multiple_of(t % (rows // step) * step, step), step)
            re = spectra_ref[d, 0, at, cols].astype(jnp.float32)
            im = spectra_ref[d, 1, at, cols].astype(jnp.float32)
            sums = []
            for e in range(beam_count):
                w_re = weight_re_ref[e, d, at, cols].astype(jnp.float32)
                w_im = weight_im_ref[e, d, at, cols].astype(jnp.float32)
                sums.append(totals[2 * e] + (w_re * re - w_im * im))
                sums.append(totals[2 * e + 1] + (w_im * re + w_re * im))
            return tuple(sums)

        zeros = tuple(jnp.zeros((step, 128), jnp.float32) for _ in range(2 * beam_count))
        totals = lax.fori_loop(0, shards * rows // step, add, zeros)
        out_ref[:, cols] = jnp.concatenate(
            [jnp.sum(total, axis=0, keepdims=True) for total in totals], axis=0
        )


def form_beams(weight_re, weight_im, spectra):
    beam_count, shards, rows, channel_count = weight_re.shape
    block = min(256, channel_count)
    weight_spec = pl.BlockSpec((beam_count, shards, rows, block), lambda k: (0, 0, 0, k))
    return pl.pallas_call(
        beam_kernel,
        grid=(channel_count // block,),
        in_specs=[
            weight_spec,
            weight_spec,
            pl.BlockSpec((shards, 2, rows, block), lambda k: (0, 0, 0, k)),
        ],
        out_specs=pl.BlockSpec((2 * beam_count, block), lambda k: (0, k)),
        out_shape=jax.ShapeDtypeStruct((2 * beam_count, channel_count), jnp.float32),
        compiler_params=pltpu.CompilerParams(vmem_limit_bytes=40 * 2**20),
        cost_estimate=pl.CostEstimate(
            flops=16 * beam_count * shards * rows * channel_count,
            bytes_accessed=4 * (beam_count + 1) * shards * rows * channel_count,
            transcendentals=0,
        ),
    )(weight_re, weight_im, spectra)


def cross_kernel(left_ref, right_ref, out_ref):
    spectra_count = left_ref.shape[1]
    left_rows = left_ref.shape[3]
    right_rows, lanes = right_ref.shape[3:]
    step = 16
    for lane in range(0, lanes, 128):
        cols = pl.ds(lane, 128)
        for row in range(0, right_rows, step):
            at = pl.ds(row, step)
            right = [
                (right_ref[0, s, 0, at, cols], right_ref[0, s, 1, at, cols])
                for s in range(spectra_count)
            ]

            def eight_rows(group, carry):
                first = pl.multiple_of(group * 8, 8)
                left = [
                    (left_ref[0, s, 0, pl.ds(first, 8), cols], left_ref[0, s, 1, pl.ds(first, 8), cols])
                    for s in range(spectra_count)
                ]
                for i in range(8):
                    re = jnp.zeros((step, 128), jnp.float32)
                    im = jnp.zeros((step, 128), jnp.float32)
                    for s in range(spectra_count):
                        l_re, l_im = left[s][0][i : i + 1], left[s][1][i : i + 1]
                        r_re, r_im = right[s]
                        re = re + (l_re * r_re + l_im * r_im)
                        im = im + (l_im * r_re - l_re * r_im)
                    out_ref[first + i, 0, 0, at, cols] = re.astype(out_ref.dtype)
                    out_ref[first + i, 0, 1, at, cols] = im.astype(out_ref.dtype)
                return carry

            lax.fori_loop(0, left_rows // 8, eight_rows, 0)


def cross_products(left, right):
    pairs, spectra_count, _, left_rows, channel_count = left.shape
    right_rows = right.shape[3]
    block = min(256, channel_count)
    return pl.pallas_call(
        cross_kernel,
        grid=(pairs, channel_count // block),
        in_specs=[
            pl.BlockSpec(
                (1, spectra_count, 2, left_rows, block), lambda b, k: (b, 0, 0, 0, k)
            ),
            pl.BlockSpec(
                (1, spectra_count, 2, right_rows, block), lambda b, k: (b, 0, 0, 0, k)
            ),
        ],
        out_specs=pl.BlockSpec((left_rows, 1, 2, right_rows, block), lambda b, k: (0, b, 0, 0, k)),
        out_shape=jax.ShapeDtypeStruct(
            (left_rows, pairs, 2, right_rows, channel_count), jnp.bfloat16
        ),
        compiler_params=pltpu.CompilerParams(vmem_limit_bytes=40 * 2**20),
    )(left, right)


def on_device(voltages, pfb_coeffs, beam_delays, slot_of_input, block_list):
    tap_count = pfb_coeffs.shape[0]
    rows_dev = voltages.shape[0]
    frame_len = pfb_coeffs.shape[1]
    spectra_dev = voltages.shape[1] // frame_len
    shards = lax.axis_size("ct") * lax.axis_size("pol")
    channel_count = NCH // shards
    inputs_all = shards * rows_dev
    half_len = FFT_B // 2
    first_table, twist_re, twist_im, second = make_tables(FFT_A, FFT_B)
    second_split = second.reshape(2, 2, shards, half_len // shards, FFT_B)

    first_channel = (
        lax.axis_index("ct") * lax.axis_size("pol") + lax.axis_index("pol")
    ) * channel_count
    channels = (first_channel + jnp.arange(channel_count, dtype=jnp.int32)).astype(jnp.float32)
    ratio = NCH / (NCH + channels)
    delays_slot = jnp.zeros_like(beam_delays).at[:, slot_of_input].set(beam_delays)
    phases = delays_slot[:, :, None] * ratio[None, None, :] * (2.0 * math.pi)
    norm_scale = inputs_all ** (-0.5)
    weight_shape = (beam_delays.shape[0], shards, rows_dev, channel_count)
    weight_re = (jnp.cos(phases) * norm_scale).astype(jnp.bfloat16).reshape(weight_shape)
    weight_im = (-jnp.sin(phases) * norm_scale).astype(jnp.bfloat16).reshape(weight_shape)

    members = jnp.arange(BLK, dtype=jnp.int32)
    needed = slot_of_input[block_list.T[:, :, None] * BLK + members].reshape(-1)
    pick = (needed[:, None] == jnp.arange(inputs_all, dtype=jnp.int32)[None, :]).astype(
        jnp.bfloat16
    )

    frames = {
        index: voltages[:, index * frame_len : (index + 1) * frame_len]
        for index in range(spectra_dev)
    }

    def channelize(taps):
        filtered = jnp.zeros((rows_dev, frame_len), jnp.float32)
        for tap_index in range(tap_count):
            filtered = filtered + pfb_coeffs[tap_index][None, :] * taps[
                tap_index
            ].astype(jnp.float32)
        shaped = filtered.astype(jnp.bfloat16).reshape(rows_dev, FFT_A, FFT_B)
        section_one = jnp.einsum(
            "ckn,rnm->rckm", first_table, shaped, preferred_element_type=jnp.float32
        )
        real_part = section_one[:, 0] * twist_re - section_one[:, 1] * twist_im
        imag_part = section_one[:, 0] * twist_im + section_one[:, 1] * twist_re
        twisted = jnp.stack([real_part, imag_part], 1).astype(jnp.bfloat16)
        outgoing = jnp.einsum(
            "ocdqm,rckm->dorqk", second_split, twisted, preferred_element_type=jnp.float32
        ).astype(jnp.bfloat16)
        return outgoing.reshape(shards, 2, rows_dev, channel_count)

    last = None
    weights = [weight_re, weight_im]
    for back in range(1, tap_count):
        own = frames[spectra_dev - back]
        if last is not None:
            own, last = lax.optimization_barrier((own, last))
        arriving = shifted(own, "tm", 1)
        if back <= 2:
            arriving, weights[back - 1] = lax.optimization_barrier((arriving, weights[back - 1]))
        last = frames[-back] = arriving

    beam_parts = [None] * spectra_dev
    gathered = [None] * spectra_dev
    outgoing = None
    for s in reversed(range(spectra_dev)):
        taps = [frames[s + tap_index - (tap_count - 1)] for tap_index in range(tap_count)]
        if outgoing is not None:
            taps, _ = lax.optimization_barrier((taps, outgoing))
        outgoing = channelize(taps)
        arrived = lax.all_to_all(outgoing, ("ct", "pol"), split_axis=0, concat_axis=0, tiled=True)
        chosen = jnp.stack(
            [
                jnp.dot(
                    pick,
                    arrived[:, part].reshape(inputs_all, channel_count),
                    preferred_element_type=jnp.float32,
                ).astype(jnp.bfloat16)
                for part in range(2)
            ]
        )
        gathered[s] = lax.all_gather(chosen, "tm", axis=0)
        beam_parts[s] = form_beams(weights[0], weights[1], arrived)

    beams = (
        jnp.stack(beam_parts)
        .reshape(spectra_dev, -1, 2, channel_count)
        .transpose(1, 0, 2, 3)
        .astype(jnp.bfloat16)
    )

    pairs = block_list.shape[0]
    steps = lax.axis_size("tm")
    rows = jnp.stack(gathered, 1).reshape(
        steps * spectra_dev, 2, 2, pairs, BLK, channel_count
    )
    own_rows = BLK // steps
    left = lax.dynamic_slice_in_dim(rows[:, :, 0], lax.axis_index("tm") * own_rows, own_rows, 3)
    left = left.transpose(2, 0, 1, 3, 4).astype(jnp.float32)
    right = rows[:, :, 1].transpose(2, 0, 1, 3, 4).astype(jnp.float32)
    return (cross_products(left, right), beams)


def solution(mesh):
    return jax.shard_map(
        on_device,
        mesh=mesh,
        in_specs=(P(("grp", "ct", "pol"), "tm"), P(), P(), P(), P()),
        out_specs=(P("tm", "grp", None, None, ("ct", "pol")), P("grp", "tm", None, ("ct", "pol"))),
        check_vma=False,
    )
```

time: 1350 us -> 625 us (0.46)
  waiting for transfers between devices: 536 us -> 280 us
  local copies, waits for them, and re-layouts: 327 us -> 79.2 us
  matrix products: 225 us -> 28 us
  other arithmetic: 218 us -> 106 us
  Pallas kernels: 0 us -> 76.4 us
  starting transfers between devices: 11.4 us -> 30.6 us
    dot_general x4 -> x12, matrix products: 225 us -> 28 us  [the longest x3 16.2 us: channelize(): jnp.einsum('ocdqm,rckm->dorqk', second_split, twisted, preferred_element_...]
    all_to_all x1 -> x3, waiting for transfers between devices: 268 us -> 81.4 us  [on_device(): lax.all_to_all(outgoing, ('ct', 'pol'), split_axis=0, concat_axis=0, tile...]
    optimization_barrier x1 -> x0, local copies, waits for them, and re-layouts: 84 us -> none  [settle(): lax.optimization_barrier(values.astype(jnp.bfloat16)).astype(jnp.float32)]
    reshape x5 -> x6, local copies, waits for them, and re-layouts: 119 us -> 41.8 us  [channelize(): return outgoing.reshape(shards, 2, rows_dev, channel_count)]
    pallas_call x0 -> x4, Pallas kernels: none -> 76.4 us  [the longest x3 45.8 us: form_beams(): pl.pallas_call(beam_kernel, grid=(channel_count // block,), in_specs=[wei...]
    ppermute x1 -> x3, waiting for transfers between devices: 268 us -> 199 us  [shifted(): return lax.ppermute(block, axis, route)]
    neg x2 -> x0, other arithmetic: 61.6 us -> none  [the longest x1 58.5 us: on_device(): -weight_im]
    another operation x1 -> x3, local copies, waits for them, and re-layouts: 56.5 us -> 0.04 us  [on_device(): jnp.stack(beam_parts).reshape(spectra_dev, -1, 2, channel_count)]
  transfers between devices with their start and end apart: 3 -> 9, of which waited for: 2 -> 4; matrix products, arithmetic and copies ran while one was open for 31% -> 25% of each run, Pallas kernels for 0% -> 7%
where the time goes in v1:
time: 625 us; the launch traced here: 615 us
  waiting for transfers between devices  280 us (45%)
  other arithmetic  106 us (17%)
  local copies, waits for them, and re-layouts  79.2 us (13%)
  Pallas kernels  76.4 us (12%)
  starting transfers between devices  30.6 us (5%)
  matrix products  28 us (4%)
  between operations  14.4 us (2%)
    ppermute x3, waiting for transfers between devices, shifted(): return lax.ppermute(block, axis, route)  199 us
    all_to_all x3, waiting for transfers between devices, on_device(): lax.all_to_all(outgoing, ('ct', 'pol'), split_axis=0, concat_axis=0, tile...  81.4 us
    convert_element_type x1, other arithmetic, on_device(): (-jnp.sin(phases) * norm_scale).astype(jnp.bfloat16).reshape(weight_shape)  65.9 us
    pallas_call x3, Pallas kernels, form_beams(): pl.pallas_call(beam_kernel, grid=(channel_count // block,), in_specs=[wei...  45.8 us
    reshape x6, local copies, waits for them, and re-layouts, channelize(): return outgoing.reshape(shards, 2, rows_dev, channel_count)  41.8 us
    pallas_call x1, Pallas kernels, cross_products(): pl.pallas_call(cross_kernel, grid=(pairs, channel_count // block), in_spe...  30.6 us
    unnamed x3, other arithmetic  19.2 us
    dot_general x3, matrix products, channelize(): jnp.einsum('ocdqm,rckm->dorqk', second_split, twisted, preferred_element_...  16.2 us
  transfers between devices with their start and end apart: 9, of which 4 were waited for; matrix products, arithmetic and copies ran while one was open for 25% of the time, Pallas kernels for 7%

profile of v1, /device:TPU:0, one launch (start us, length us, event | category | flops | bytes accessed | tf_op | source)
XLA Modules:
  0.0 615.1 jit_solution(9118002672604670936)
XLA Ops:
  7.2 9.1 %fusion.61 = (bf16[128,16384]{1,0:T(8,128)(2,1)}, bf16[128,16384]{1,0:T(8,128)(2,1)}, bf16[128,16384]{1,0:T(8,128)(2,1)}) fusion(bf16[128,49152]{1,0:T(8,128)(2,1)} %param.5), kind=kLoop, calls=%fused_computation.120 | loop fusion | bytes 25165824 | tf_op jit(solution)/shard_map/slice | solution.py:186
  16.2 6.8 %collective-permute-start = (bf16[128,16384]{1,0:T(8,128)(2,1)}, bf16[128,16384]{1,0:T(8,128)(2,1)}, u32[]{:S(2)}, u32[]{:S(2)}) collective-permute-start(bf16[128,16384]{1,0:T(8,128)(2,1)} %get-tuple-element.37), channel_id=1, source_target_pairs={{0,2},{1,3},{4,6},{5,7},{8,10},{9,11},{12,14},{13,15},{16,18},{17,... | collective-permute-start | bytes 12582920 | tf_op jit(solution)/shard_map/ppermute | solution.py:19
  23.3 3.2 scatter_custom_fusion
  26.7 65.9 %multiply_convert_fusion = (bf16[4,8,128,1024]{3,2,1,0:T(8,128)(2,1)}, bf16[4,8,128,1024]{3,2,1,0:T(8,128)(2,1)}) fusion(f32[1024]{0:T(1024)S(1)} %add_divide_fusion, f32[4,8,128]{2,1,0:T(8,128)S(1)} %copy.44), kind=kLoop, calls=%fused_computation.2 | loop fusion | flops 29360128 | bytes 16797696 | tf_op jit(solution)/shard_map/convert_element_type | solution.py:177
  93.6 17.6 %collective-permute-done = bf16[128,16384]{1,0:T(8,128)(2,1)} collective-permute-done((bf16[128,16384]{1,0:T(8,128)(2,1)}, bf16[128,16384]{1,0:T(8,128)(2,1)}, u32[]{:S(2)}, u32[]{:S(2)}) %collective-permute-start) | collective-permute-done | bytes 4194336 | tf_op jit(solution)/shard_map/ppermute | solution.py:19
  111.2 4.9 fusion.9
  116.1 1.2 copy.86
  117.4 2.4 convolution_bitcast_fusion.2
  119.7 3.9 subtract_convert_fusion.2
  123.6 5.4 fusion.12
  129.1 7.6 %reshape.323 = bf16[8,2,128,1024]{3,0,1,2:T(8,128)(2,1)} reshape(bf16[8,2,128,8,128]{4,3,0,1,2:T(8,128)(2,1)} %fusion.12) | data formatting | bytes 8388608 | tf_op jit(solution)/shard_map/reshape | solution.py:206
  136.7 6.6 %copy.72 = bf16[8,2,128,1024]{3,2,1,0:T(8,128)(2,1)} copy(bf16[8,2,128,1024]{3,0,1,2:T(8,128)(2,1)} %reshape.323) | data formatting | bytes 8388608 | tf_op jit(solution)/shard_map/reshape | solution.py:206
  143.2 4.9 all-to-all-start.2
  148.1 4.6 collective-permute-start.1
  152.8 90.5 %collective-permute-done.1 = bf16[128,16384]{1,0:T(8,128)(2,1)S(1)} collective-permute-done((bf16[128,16384]{1,0:T(8,128)(2,1)}, bf16[128,16384]{1,0:T(8,128)(2,1)S(1)}, u32[]{:S(2)}, u32[]{:S(2)}) %collective-permute-start.1) | collective-permute-done | bytes 4194336 | tf_op jit(solution)/shard_map/ppermute | solution.py:19
  243.3 7.8 %fusion.10 = bf16[16,8,128,128]{3,1,2,0:T(8,128)(2,1)S(1)} fusion(bf16[128,16384]{1,0:T(8,128)(2,1)} %get-tuple-element.23, bf16[128,16384]{1,0:T(8,128)(2,1)} %get-tuple-element.27, bf16[128,16384]{1,0:T(8,128)(2,1)} %collective-permute-done, bf16[128,16384]{1,0:T(8,128)(2,1)S(1)} %collective-permute-done.1, f32[16384]{0:T(1024)S(1)} %bitcast.172, ...), kind=kLoop, calls=%fused_computation.35 | loop fusion | flops 25165824 | bytes 21233664
  251.1 1.2 copy.87
  252.4 2.4 convolution_bitcast_fusion.1
  254.8 3.9 subtract_convert_fusion.1
  258.7 5.5 fusion.13
  264.1 7.3 %reshape.324 = bf16[8,2,128,1024]{3,0,1,2:T(8,128)(2,1)} reshape(bf16[8,2,128,8,128]{4,3,0,1,2:T(8,128)(2,1)} %fusion.13) | data formatting | bytes 8388608 | tf_op jit(solution)/shard_map/reshape | solution.py:206
  271.4 6.5 %copy.77 = bf16[8,2,128,1024]{3,2,1,0:T(8,128)(2,1)} copy(bf16[8,2,128,1024]{3,0,1,2:T(8,128)(2,1)} %reshape.324) | data formatting | bytes 8388608 | tf_op jit(solution)/shard_map/reshape | solution.py:206
  277.9 4.7 all-to-all-start.1
  282.7 4.5 collective-permute-start.2
  287.2 90.5 %collective-permute-done.2 = bf16[128,16384]{1,0:T(8,128)(2,1)S(1)} collective-permute-done((bf16[128,16384]{1,0:T(8,128)(2,1)}, bf16[128,16384]{1,0:T(8,128)(2,1)S(1)}, u32[]{:S(2)}, u32[]{:S(2)}) %collective-permute-start.2) | collective-permute-done | bytes 4194336 | tf_op jit(solution)/shard_map/ppermute | solution.py:19
  377.8 6.5 %fusion.11 = bf16[16,8,128,128]{3,1,2,0:T(8,128)(2,1)S(1)} fusion(bf16[128,16384]{1,0:T(8,128)(2,1)} %get-tuple-element.27, bf16[128,16384]{1,0:T(8,128)(2,1)} %collective-permute-done, bf16[128,16384]{1,0:T(8,128)(2,1)} %copy-done.5, bf16[128,16384]{1,0:T(8,128)(2,1)S(1)} %collective-permute-done.2, f32[16384]{0:T(1024)S(1)} %bitcast.173, ...), kind=kLoop, calls=%fused_computation.36 | loop fusion | flops 25165824 | bytes 21233664
  384.2 1.2 copy.88
  385.5 2.4 convolution_bitcast_fusion
  387.9 3.9 subtract_convert_fusion
  391.7 5.4 fusion.14
  397.1 7.3 %reshape.325 = bf16[8,2,128,1024]{3,0,1,2:T(8,128)(2,1)} reshape(bf16[8,2,128,8,128]{4,3,0,1,2:T(8,128)(2,1)} %fusion.14) | data formatting | bytes 8388608 | tf_op jit(solution)/shard_map/reshape | solution.py:206
  404.4 6.5 %copy.82 = bf16[8,2,128,1024]{3,2,1,0:T(8,128)(2,1)} copy(bf16[8,2,128,1024]{3,0,1,2:T(8,128)(2,1)} %reshape.325) | data formatting | bytes 8388608 | tf_op jit(solution)/shard_map/reshape | solution.py:206
  410.9 4.9 all-to-all-start
  416.1 1.6 gather_fusion
  417.7 2.7 fusion.65
  423.1 2.7 fusion.64
  427.3 1.1 pad_maximum_fusion.2
  428.5 81.4 %all-to-all-done.spectra_ref = bf16[8,2,128,1024]{3,2,1,0:T(8,128)(2,1)} async-done(((bf16[8,2,128,1024]{3,2,1,0:T(8,128)(2,1)}), bf16[8,2,128,1024]{3,2,1,0:T(8,128)(2,1)}, u32[]{:S(2)}, u32[]{:S(2)}) %all-to-all-start) | async-done | bytes 4194336 | tf_op jit(solution)/shard_map/all_to_all | solution.py:227
  509.9 2.7 fusion.63
  514.1 1.1 pad_maximum_fusion.1
  515.3 3.4 copy-done
  518.6 15.3 %shard_map.71 = f32[8,1024]{1,0:T(8,128)S(1)} custom-call(bf16[4,8,128,1024]{3,2,1,0:T(8,128)(2,1)S(1)} %copy-done, bf16[4,8,128,1024]{3,2,1,0:T(8,128)(2,1)} %get-tuple-element.29.weight_im_ref, bf16[8,2,128,1024]{3,2,1,0:T(8,128)(2,1)} %all-to-all-done.2.spectra_ref), custom_call_target="tpu_custom_call" | custom-call | flops 67108864 | bytes 20971520 | tf_op jit(solution)/shard_map/pallas_call | solution.py:78
  533.9 3.4 copy-done.1
  537.3 15.3 %shard_map.70 = f32[8,1024]{1,0:T(8,128)S(1)} custom-call(bf16[4,8,128,1024]{3,2,1,0:T(8,128)(2,1)S(1)} %copy-done.1, bf16[4,8,128,1024]{3,2,1,0:T(8,128)(2,1)} %get-tuple-element.29.weight_im_ref, bf16[8,2,128,1024]{3,2,1,0:T(8,128)(2,1)} %all-to-all-done.1.spectra_ref), custom_call_target="tpu_custom_call" | custom-call | flops 67108864 | bytes 20971520 | tf_op jit(solution)/shard_map/pallas_call | solution.py:78
  552.6 3.4 copy-done.2
  556.0 15.3 %shard_map.69 = f32[8,1024]{1,0:T(8,128)S(1)} custom-call(bf16[4,8,128,1024]{3,2,1,0:T(8,128)(2,1)S(1)} %copy-done.2, bf16[4,8,128,1024]{3,2,1,0:T(8,128)(2,1)} %get-tuple-element.29.weight_im_ref, bf16[8,2,128,1024]{3,2,1,0:T(8,128)(2,1)} %all-to-all-done.spectra_ref), custom_call_target="tpu_custom_call" | custom-call | flops 67108864 | bytes 20971520 | tf_op jit(solution)/shard_map/pallas_call | solution.py:78
  572.0 3.7 pad_maximum_fusion
  577.7 30.6 %shard_map.68 = bf16[32,2,2,64,1024]{4,3,2,1,0:T(8,128)(2,1)} custom-call(f32[2,6,2,32,1024]{4,3,2,1,0:T(8,128)S(1)} %convert_bitcast_fusion.1.left_ref, f32[2,6,2,64,1024]{4,3,2,1,0:T(8,128)S(1)} %convert_bitcast_fusion.right_ref), custom_call_target="tpu_custom_call" | custom-call | tf_op jit(solution)/shard_map/pallas_call | solution.py:136
  (57 shorter events, 10.3 us)
Async XLA Ops:
  7.2 15.9 %copy-start.7 = (f32[4,1024]{1,0:T(4,128)S(1)}, f32[4,1024]{1,0:T(4,128)}, u32[]{:S(2)}) copy-start(f32[4,1024]{1,0:T(4,128)} %param.7) | copy-start | bytes 49156
  7.2 16.1 %copy-start.3 = (s32[1024]{0:T(1024)S(1)}, s32[1024]{0:T(1024)}, u32[]{:S(2)}) copy-start(s32[1024]{0:T(1024)} %param.8) | copy-start | bytes 12292
  16.2 95.0 %collective-permute-start = (bf16[128,16384]{1,0:T(8,128)(2,1)}, bf16[128,16384]{1,0:T(8,128)(2,1)}, u32[]{:S(2)}, u32[]{:S(2)}) collective-permute-start(bf16[128,16384]{1,0:T(8,128)(2,1)} %get-tuple-element.37), channel_id=1, source_target_pairs={{0,2},{1,3},{4,6},{5,7},{8,10},{9,11},{12,14},{13,15},{16,18},{17,... | collective-permute-start | bytes 12582920 | tf_op jit(solution)/shard_map/ppermute | solution.py:19
  26.7 66.7 %copy-start.6 = (f32[4,16384]{1,0:T(4,128)S(1)}, f32[4,16384]{1,0:T(4,128)}, u32[]{:S(2)}) copy-start(f32[4,16384]{1,0:T(4,128)} %param.6) | copy-start | bytes 786436
  26.7 84.5 %copy-start.4 = (bf16[128,49152]{1,0:T(8,128)(2,1)S(1)}, bf16[128,49152]{1,0:T(8,128)(2,1)}, u32[]{:S(2)}) copy-start(bf16[128,49152]{1,0:T(8,128)(2,1)} %param.5) | copy-start | bytes 37748740
  143.2 134.7 %all-to-all-start.2 = ((bf16[8,2,128,1024]{3,2,1,0:T(8,128)(2,1)}), bf16[8,2,128,1024]{3,2,1,0:T(8,128)(2,1)}, u32[]{:S(2)}, u32[]{:S(2)}) async-start(bf16[8,2,128,1024]{3,2,1,0:T(8,128)(2,1)} %copy.72), calls=%async_computation.2 | async-start | bytes 8388608 | tf_op jit(solution)/shard_map/all_to_all | solution.py:227
  148.1 95.2 %collective-permute-start.1 = (bf16[128,16384]{1,0:T(8,128)(2,1)}, bf16[128,16384]{1,0:T(8,128)(2,1)S(1)}, u32[]{:S(2)}, u32[]{:S(2)}) collective-permute-start(bf16[128,16384]{1,0:T(8,128)(2,1)} %get-tuple-element.23), channel_id=1, source_target_pairs={{0,2},{1,3},{4,6},{5,7},{8,10},{9,11},{12,14},{13,15},{16,18},{17,... | collective-permute-start | bytes 12582920 | tf_op jit(solution)/shard_map/ppermute | solution.py:19
  243.3 7.8 %copy-start.5 = (bf16[128,16384]{1,0:T(8,128)(2,1)}, bf16[128,16384]{1,0:T(8,128)(2,1)S(1)}, u32[]{:S(2)}) copy-start(bf16[128,16384]{1,0:T(8,128)(2,1)S(1)} %collective-permute-done.1) | copy-start | bytes 12582916
  277.9 132.9 %all-to-all-start.1 = ((bf16[8,2,128,1024]{3,2,1,0:T(8,128)(2,1)}), bf16[8,2,128,1024]{3,2,1,0:T(8,128)(2,1)}, u32[]{:S(2)}, u32[]{:S(2)}) async-start(bf16[8,2,128,1024]{3,2,1,0:T(8,128)(2,1)} %copy.77), calls=%async_computation.1 | async-start | bytes 8388608 | tf_op jit(solution)/shard_map/all_to_all | solution.py:227
  282.7 95.1 %collective-permute-start.2 = (bf16[128,16384]{1,0:T(8,128)(2,1)}, bf16[128,16384]{1,0:T(8,128)(2,1)S(1)}, u32[]{:S(2)}, u32[]{:S(2)}) collective-permute-start(bf16[128,16384]{1,0:T(8,128)(2,1)} %get-tuple-element.27), channel_id=1, source_target_pairs={{0,2},{1,3},{4,6},{5,7},{8,10},{9,11},{12,14},{13,15},{16,18},{17,... | collective-permute-start | bytes 12582920 | tf_op jit(solution)/shard_map/ppermute | solution.py:19
  410.9 4.9 copy-start.8
  410.9 99.0 %all-to-all-start = ((bf16[8,2,128,1024]{3,2,1,0:T(8,128)(2,1)}), bf16[8,2,128,1024]{3,2,1,0:T(8,128)(2,1)}, u32[]{:S(2)}, u32[]{:S(2)}) async-start(bf16[8,2,128,1024]{3,2,1,0:T(8,128)(2,1)} %copy.82), calls=%async_computation | async-start | bytes 8388608 | tf_op jit(solution)/shard_map/all_to_all | solution.py:227
  415.8 156.3 %all-gather.11.cloned.1.call-start = ((), (), s32[]{:S(2)}) async-start(), calls=%async_computation.5 | async-start | bytes 3145728 | tf_op jit(solution)/shard_map/all_gather | solution.py:238
  423.0 149.0 %all-gather.9.cloned.1.call-start = ((), (), s32[]{:S(2)}) async-start(), calls=%async_computation.4 | async-start | bytes 3145728 | tf_op jit(solution)/shard_map/all_gather | solution.py:238
  428.5 143.6 %all-gather.7.cloned.1.call-start = ((), (), s32[]{:S(2)}) async-start(), calls=%async_computation.3 | async-start | bytes 3145728 | tf_op jit(solution)/shard_map/all_gather | solution.py:238
  515.2 3.4 copy-start
  533.9 3.4 copy-start.1
  552.6 3.4 copy-start.2
Sparse Core Ops, SparseCore 0:
  423.2 35.4 all-gather.10
  460.2 33.1 all-gather.8
  515.4 32.9 all-gather.6

commit v2 on v1

--- a/solution.py
+++ b/solution.py
@@ -225,6 +225,8 @@
             taps, _ = lax.optimization_barrier((taps, outgoing))
         outgoing = channelize(taps)
         arrived = lax.all_to_all(outgoing, ("ct", "pol"), split_axis=0, concat_axis=0, tiled=True)
+        if s + 1 < spectra_dev:
+            arrived, beam_parts[s + 1] = lax.optimization_barrier((arrived, beam_parts[s + 1]))
         chosen = jnp.stack(
             [
                 jnp.dot(

time: 625 us -> 602 us (0.963)
  waiting for transfers between devices: 280 us -> 256 us
    all_to_all x3, waiting for transfers between devices: 81.4 us -> 44.1 us  [on_device(): lax.all_to_all(outgoing, ('ct', 'pol'), split_axis=0, concat_axis=0, tile...]
    all_gather x3, waiting for transfers between devices: 0.01 us -> 13.6 us  [on_device(): gathered[s] = lax.all_gather(chosen, 'tm', axis=0)]
  transfers between devices with their start and end apart: 9 -> 9, of which waited for: 4 -> 5; matrix products, arithmetic and copies ran while one was open for 25% -> 27% of each run, Pallas kernels for 7% -> 8%
where the time goes in v2:
time: 602 us; the launch traced here: 591 us
  waiting for transfers between devices  256 us (43%)
  other arithmetic  106 us (18%)
  local copies, waits for them, and re-layouts  79.2 us (13%)
  Pallas kernels  76.4 us (13%)
  starting transfers between devices  30.6 us (5%)
  matrix products  28 us (5%)
  between operations  14.4 us (2%)
    ppermute x3, waiting for transfers between devices, shifted(): return lax.ppermute(block, axis, route)  199 us
    convert_element_type x1, other arithmetic, on_device(): (-jnp.sin(phases) * norm_scale).astype(jnp.bfloat16).reshape(weight_shape)  65.9 us
    pallas_call x3, Pallas kernels, form_beams(): pl.pallas_call(beam_kernel, grid=(channel_count // block,), in_specs=[wei...  45.8 us
    all_to_all x3, waiting for transfers between devices, on_device(): lax.all_to_all(outgoing, ('ct', 'pol'), split_axis=0, concat_axis=0, tile...  44.1 us
    reshape x6, local copies, waits for them, and re-layouts, channelize(): return outgoing.reshape(shards, 2, rows_dev, channel_count)  41.8 us
    pallas_call x1, Pallas kernels, cross_products(): pl.pallas_call(cross_kernel, grid=(pairs, channel_count // block), in_spe...  30.6 us
    unnamed x3, other arithmetic  19.2 us
    dot_general x3, matrix products, channelize(): jnp.einsum('ocdqm,rckm->dorqk', second_split, twisted, preferred_element_...  16.2 us
  transfers between devices with their start and end apart: 9, of which 5 were waited for; matrix products, arithmetic and copies ran while one was open for 27% of the time, Pallas kernels for 8%

profile of v2, /device:TPU:0, one launch (start us, length us, event | category | flops | bytes accessed | tf_op | source)
XLA Modules:
  0.0 591.3 jit_solution(11950853322278449303)
XLA Ops:
  7.2 9.1 %fusion.61 = (bf16[128,16384]{1,0:T(8,128)(2,1)}, bf16[128,16384]{1,0:T(8,128)(2,1)}, bf16[128,16384]{1,0:T(8,128)(2,1)}) fusion(bf16[128,49152]{1,0:T(8,128)(2,1)} %param.5), kind=kLoop, calls=%fused_computation.120 | loop fusion | bytes 25165824 | tf_op jit(solution)/shard_map/slice | solution.py:186
  16.2 6.8 %collective-permute-start = (bf16[128,16384]{1,0:T(8,128)(2,1)}, bf16[128,16384]{1,0:T(8,128)(2,1)}, u32[]{:S(2)}, u32[]{:S(2)}) collective-permute-start(bf16[128,16384]{1,0:T(8,128)(2,1)} %get-tuple-element.45), channel_id=1, source_target_pairs={{0,2},{1,3},{4,6},{5,7},{8,10},{9,11},{12,14},{13,15},{16,18},{17,... | collective-permute-start | bytes 12582920 | tf_op jit(solution)/shard_map/ppermute | solution.py:19
  23.3 3.2 scatter_custom_fusion
  26.7 65.9 %multiply_convert_fusion = (bf16[4,8,128,1024]{3,2,1,0:T(8,128)(2,1)}, bf16[4,8,128,1024]{3,2,1,0:T(8,128)(2,1)}) fusion(f32[1024]{0:T(1024)S(1)} %add_divide_fusion, f32[4,8,128]{2,1,0:T(8,128)S(1)} %copy.44), kind=kLoop, calls=%fused_computation.2 | loop fusion | flops 29360128 | bytes 16797696 | tf_op jit(solution)/shard_map/convert_element_type | solution.py:177
  93.6 17.6 %collective-permute-done = bf16[128,16384]{1,0:T(8,128)(2,1)} collective-permute-done((bf16[128,16384]{1,0:T(8,128)(2,1)}, bf16[128,16384]{1,0:T(8,128)(2,1)}, u32[]{:S(2)}, u32[]{:S(2)}) %collective-permute-start) | collective-permute-done | bytes 4194336 | tf_op jit(solution)/shard_map/ppermute | solution.py:19
  111.2 4.9 fusion.9
  116.1 1.2 copy.86
  117.4 2.4 convolution_bitcast_fusion.2
  119.7 3.9 subtract_convert_fusion.2
  123.6 5.4 fusion.12
  129.1 7.6 %reshape.323 = bf16[8,2,128,1024]{3,0,1,2:T(8,128)(2,1)} reshape(bf16[8,2,128,8,128]{4,3,0,1,2:T(8,128)(2,1)} %fusion.12) | data formatting | bytes 8388608 | tf_op jit(solution)/shard_map/reshape | solution.py:206
  136.7 6.6 %copy.72 = bf16[8,2,128,1024]{3,2,1,0:T(8,128)(2,1)} copy(bf16[8,2,128,1024]{3,0,1,2:T(8,128)(2,1)} %reshape.323) | data formatting | bytes 8388608 | tf_op jit(solution)/shard_map/reshape | solution.py:206
  143.2 4.9 all-to-all-start.2
  148.1 4.6 collective-permute-start.1
  152.8 90.5 %collective-permute-done.1 = bf16[128,16384]{1,0:T(8,128)(2,1)S(1)} collective-permute-done((bf16[128,16384]{1,0:T(8,128)(2,1)}, bf16[128,16384]{1,0:T(8,128)(2,1)S(1)}, u32[]{:S(2)}, u32[]{:S(2)}) %collective-permute-start.1) | collective-permute-done | bytes 4194336 | tf_op jit(solution)/shard_map/ppermute | solution.py:19
  243.3 7.8 %fusion.10 = bf16[16,8,128,128]{3,1,2,0:T(8,128)(2,1)S(1)} fusion(bf16[128,16384]{1,0:T(8,128)(2,1)} %get-tuple-element.27, bf16[128,16384]{1,0:T(8,128)(2,1)} %get-tuple-element.31, bf16[128,16384]{1,0:T(8,128)(2,1)} %collective-permute-done, bf16[128,16384]{1,0:T(8,128)(2,1)S(1)} %collective-permute-done.1, f32[16384]{0:T(1024)S(1)} %bitcast.172, ...), kind=kLoop, calls=%fused_computation.35 | loop fusion | flops 25165824 | bytes 21233664
  251.1 1.2 copy.87
  252.4 2.4 convolution_bitcast_fusion.1
  254.8 3.9 subtract_convert_fusion.1
  258.7 5.5 fusion.13
  264.1 7.3 %reshape.324 = bf16[8,2,128,1024]{3,0,1,2:T(8,128)(2,1)} reshape(bf16[8,2,128,8,128]{4,3,0,1,2:T(8,128)(2,1)} %fusion.13) | data formatting | bytes 8388608 | tf_op jit(solution)/shard_map/reshape | solution.py:206
  271.4 6.5 %copy.77 = bf16[8,2,128,1024]{3,2,1,0:T(8,128)(2,1)} copy(bf16[8,2,128,1024]{3,0,1,2:T(8,128)(2,1)} %reshape.324) | data formatting | bytes 8388608 | tf_op jit(solution)/shard_map/reshape | solution.py:206
  277.9 4.7 all-to-all-start.1
  282.7 4.5 collective-permute-start.2
  287.2 90.5 %collective-permute-done.2 = bf16[128,16384]{1,0:T(8,128)(2,1)S(1)} collective-permute-done((bf16[128,16384]{1,0:T(8,128)(2,1)}, bf16[128,16384]{1,0:T(8,128)(2,1)S(1)}, u32[]{:S(2)}, u32[]{:S(2)}) %collective-permute-start.2) | collective-permute-done | bytes 4194336 | tf_op jit(solution)/shard_map/ppermute | solution.py:19
  377.8 6.5 %fusion.11 = bf16[16,8,128,128]{3,1,2,0:T(8,128)(2,1)S(1)} fusion(bf16[128,16384]{1,0:T(8,128)(2,1)} %get-tuple-element.31, bf16[128,16384]{1,0:T(8,128)(2,1)} %collective-permute-done, bf16[128,16384]{1,0:T(8,128)(2,1)} %copy-done.5, bf16[128,16384]{1,0:T(8,128)(2,1)S(1)} %collective-permute-done.2, f32[16384]{0:T(1024)S(1)} %bitcast.173, ...), kind=kLoop, calls=%fused_computation.36 | loop fusion | flops 25165824 | bytes 21233664
  384.2 1.2 copy.88
  385.5 2.4 convolution_bitcast_fusion
  387.9 3.9 subtract_convert_fusion
  391.7 5.4 fusion.14
  397.1 7.3 %reshape.325 = bf16[8,2,128,1024]{3,0,1,2:T(8,128)(2,1)} reshape(bf16[8,2,128,8,128]{4,3,0,1,2:T(8,128)(2,1)} %fusion.14) | data formatting | bytes 8388608 | tf_op jit(solution)/shard_map/reshape | solution.py:206
  404.4 6.5 %copy.82 = bf16[8,2,128,1024]{3,2,1,0:T(8,128)(2,1)} copy(bf16[8,2,128,1024]{3,0,1,2:T(8,128)(2,1)} %reshape.325) | data formatting | bytes 8388608 | tf_op jit(solution)/shard_map/reshape | solution.py:206
  410.9 4.9 all-to-all-start
  416.1 1.6 gather_fusion
  417.7 2.7 fusion.65
  423.1 3.4 copy-done
  426.5 15.3 %shard_map.68 = f32[8,1024]{1,0:T(8,128)S(1)} custom-call(bf16[4,8,128,1024]{3,2,1,0:T(8,128)(2,1)S(1)} %copy-done, bf16[4,8,128,1024]{3,2,1,0:T(8,128)(2,1)} %get-tuple-element.33.weight_im_ref, bf16[8,2,128,1024]{3,2,1,0:T(8,128)(2,1)} %all-to-all-done.2.spectra_ref), custom_call_target="tpu_custom_call" | custom-call | flops 67108864 | bytes 20971520 | tf_op jit(solution)/shard_map/pallas_call | solution.py:78
  441.7 2.7 fusion.64
  446.0 1.1 pad_maximum_fusion.2
  447.2 3.4 copy-done.1
  450.6 15.3 %shard_map.69 = f32[8,1024]{1,0:T(8,128)S(1)} custom-call(bf16[4,8,128,1024]{3,2,1,0:T(8,128)(2,1)S(1)} %copy-done.1, bf16[4,8,128,1024]{3,2,1,0:T(8,128)(2,1)} %get-tuple-element.33.weight_im_ref, bf16[8,2,128,1024]{3,2,1,0:T(8,128)(2,1)} %all-to-all-done.1.spectra_ref), custom_call_target="tpu_custom_call" | custom-call | flops 67108864 | bytes 20971520 | tf_op jit(solution)/shard_map/pallas_call | solution.py:78
  465.8 44.1 %all-to-all-done.spectra_ref = bf16[8,2,128,1024]{3,2,1,0:T(8,128)(2,1)} async-done(((bf16[8,2,128,1024]{3,2,1,0:T(8,128)(2,1)}), bf16[8,2,128,1024]{3,2,1,0:T(8,128)(2,1)}, u32[]{:S(2)}, u32[]{:S(2)}) %all-to-all-start) | async-done | bytes 4194336 | tf_op jit(solution)/shard_map/all_to_all | solution.py:227
  509.9 2.7 fusion.63
  515.3 3.4 copy-done.2
  518.6 15.3 %shard_map.71 = f32[8,1024]{1,0:T(8,128)S(1)} custom-call(bf16[4,8,128,1024]{3,2,1,0:T(8,128)(2,1)S(1)} %copy-done.2, bf16[4,8,128,1024]{3,2,1,0:T(8,128)(2,1)} %get-tuple-element.33.weight_im_ref, bf16[8,2,128,1024]{3,2,1,0:T(8,128)(2,1)} %all-to-all-done.spectra_ref), custom_call_target="tpu_custom_call" | custom-call | flops 67108864 | bytes 20971520 | tf_op jit(solution)/shard_map/pallas_call | solution.py:78
  534.7 13.6 %all-gather.7.cloned.1.call-done = bf16[4,256,1024]{2,1,0:T(8,128)(2,1)} async-done(((bf16[2,256,1024]{2,1,0:T(8,128)(2,1)}), bf16[4,256,1024]{2,1,0:T(8,128)(2,1)}) %all-gather.7.cloned.1.call-update) | async-done | bytes 2097168 | tf_op jit(solution)/shard_map/all_gather | solution.py:240
  548.3 3.7 pad_maximum_fusion
  554.0 30.6 %shard_map.70 = bf16[32,2,2,64,1024]{4,3,2,1,0:T(8,128)(2,1)} custom-call(f32[2,6,2,32,1024]{4,3,2,1,0:T(8,128)S(1)} %convert_bitcast_fusion.1.left_ref, f32[2,6,2,64,1024]{4,3,2,1,0:T(8,128)S(1)} %convert_bitcast_fusion.right_ref), custom_call_target="tpu_custom_call" | custom-call | tf_op jit(solution)/shard_map/pallas_call | solution.py:136
  (57 shorter events, 11.3 us)
Async XLA Ops:
  7.2 15.9 %copy-start.7 = (f32[4,1024]{1,0:T(4,128)S(1)}, f32[4,1024]{1,0:T(4,128)}, u32[]{:S(2)}) copy-start(f32[4,1024]{1,0:T(4,128)} %param.7) | copy-start | bytes 49156
  7.2 16.1 %copy-start.3 = (s32[1024]{0:T(1024)S(1)}, s32[1024]{0:T(1024)}, u32[]{:S(2)}) copy-start(s32[1024]{0:T(1024)} %param.8) | copy-start | bytes 12292
  16.2 95.0 %collective-permute-start = (bf16[128,16384]{1,0:T(8,128)(2,1)}, bf16[128,16384]{1,0:T(8,128)(2,1)}, u32[]{:S(2)}, u32[]{:S(2)}) collective-permute-start(bf16[128,16384]{1,0:T(8,128)(2,1)} %get-tuple-element.45), channel_id=1, source_target_pairs={{0,2},{1,3},{4,6},{5,7},{8,10},{9,11},{12,14},{13,15},{16,18},{17,... | collective-permute-start | bytes 12582920 | tf_op jit(solution)/shard_map/ppermute | solution.py:19
  26.7 66.7 %copy-start.6 = (f32[4,16384]{1,0:T(4,128)S(1)}, f32[4,16384]{1,0:T(4,128)}, u32[]{:S(2)}) copy-start(f32[4,16384]{1,0:T(4,128)} %param.6) | copy-start | bytes 786436
  26.7 84.5 %copy-start.4 = (bf16[128,49152]{1,0:T(8,128)(2,1)S(1)}, bf16[128,49152]{1,0:T(8,128)(2,1)}, u32[]{:S(2)}) copy-start(bf16[128,49152]{1,0:T(8,128)(2,1)} %param.5) | copy-start | bytes 37748740
  143.2 134.7 %all-to-all-start.2 = ((bf16[8,2,128,1024]{3,2,1,0:T(8,128)(2,1)}), bf16[8,2,128,1024]{3,2,1,0:T(8,128)(2,1)}, u32[]{:S(2)}, u32[]{:S(2)}) async-start(bf16[8,2,128,1024]{3,2,1,0:T(8,128)(2,1)} %copy.72), calls=%async_computation.2 | async-start | bytes 8388608 | tf_op jit(solution)/shard_map/all_to_all | solution.py:227
  148.1 95.2 %collective-permute-start.1 = (bf16[128,16384]{1,0:T(8,128)(2,1)}, bf16[128,16384]{1,0:T(8,128)(2,1)S(1)}, u32[]{:S(2)}, u32[]{:S(2)}) collective-permute-start(bf16[128,16384]{1,0:T(8,128)(2,1)} %get-tuple-element.27), channel_id=1, source_target_pairs={{0,2},{1,3},{4,6},{5,7},{8,10},{9,11},{12,14},{13,15},{16,18},{17,... | collective-permute-start | bytes 12582920 | tf_op jit(solution)/shard_map/ppermute | solution.py:19
  243.3 7.8 %copy-start.5 = (bf16[128,16384]{1,0:T(8,128)(2,1)}, bf16[128,16384]{1,0:T(8,128)(2,1)S(1)}, u32[]{:S(2)}) copy-start(bf16[128,16384]{1,0:T(8,128)(2,1)S(1)} %collective-permute-done.1) | copy-start | bytes 12582916
  277.9 132.9 %all-to-all-start.1 = ((bf16[8,2,128,1024]{3,2,1,0:T(8,128)(2,1)}), bf16[8,2,128,1024]{3,2,1,0:T(8,128)(2,1)}, u32[]{:S(2)}, u32[]{:S(2)}) async-start(bf16[8,2,128,1024]{3,2,1,0:T(8,128)(2,1)} %copy.77), calls=%async_computation.1 | async-start | bytes 8388608 | tf_op jit(solution)/shard_map/all_to_all | solution.py:227
  282.7 95.1 %collective-permute-start.2 = (bf16[128,16384]{1,0:T(8,128)(2,1)}, bf16[128,16384]{1,0:T(8,128)(2,1)S(1)}, u32[]{:S(2)}, u32[]{:S(2)}) collective-permute-start(bf16[128,16384]{1,0:T(8,128)(2,1)} %get-tuple-element.31), channel_id=1, source_target_pairs={{0,2},{1,3},{4,6},{5,7},{8,10},{9,11},{12,14},{13,15},{16,18},{17,... | collective-permute-start | bytes 12582920 | tf_op jit(solution)/shard_map/ppermute | solution.py:19
  410.9 4.9 copy-start.8
  410.9 99.0 %all-to-all-start = ((bf16[8,2,128,1024]{3,2,1,0:T(8,128)(2,1)}), bf16[8,2,128,1024]{3,2,1,0:T(8,128)(2,1)}, u32[]{:S(2)}, u32[]{:S(2)}) async-start(bf16[8,2,128,1024]{3,2,1,0:T(8,128)(2,1)} %copy.82), calls=%async_computation | async-start | bytes 8388608 | tf_op jit(solution)/shard_map/all_to_all | solution.py:227
  415.8 119.0 %all-gather.11.cloned.1.call-start = ((), (), s32[]{:S(2)}) async-start(), calls=%async_computation.5 | async-start | bytes 3145728 | tf_op jit(solution)/shard_map/all_gather | solution.py:240
  423.0 111.7 %all-gather.9.cloned.1.call-start = ((), (), s32[]{:S(2)}) async-start(), calls=%async_computation.4 | async-start | bytes 3145728 | tf_op jit(solution)/shard_map/all_gather | solution.py:240
  423.1 3.4 copy-start
  447.1 101.2 %all-gather.7.cloned.1.call-start = ((), (), s32[]{:S(2)}) async-start(), calls=%async_computation.3 | async-start | bytes 3145728 | tf_op jit(solution)/shard_map/all_gather | solution.py:240
  447.2 3.4 copy-start.1
  515.3 3.4 copy-start.2
Sparse Core Ops, SparseCore 0:
  423.1 35.4 all-gather.10
  460.2 33.1 all-gather.8
  515.3 32.9 all-gather.6
